TPU v7x, 256 devices: a whole 4x4x8 slice. The times are simulated.
256 devices in a mesh: dp: 64 (over z, x, core), tensor: 4 (over y).
Axes of the slice: x: 4, y: 4, z: 8, core: 2. Of those that a mesh axis runs over, the one named last changes fastest.
Arguments:
- hidden_acts: bfloat16 [64, 768, 896], P('dp', None, 'tensor'), may hold values from -6 to 6
- out_grads: bfloat16 [768, 16384], P('dp', 'tensor'), may hold values from -0.21875 to 0.21875
- residual_in: bfloat16 [64, 896, 8192], P('dp', 'tensor'), may hold values from -6 to 6
- q_prev: bfloat16 [8192, 32], replicated, may hold values from -0.0625 to 0.0625
Outputs:
- p_basis: float32 [28672, 32], P('tensor')
- q_new: float32 [8192, 32], P('dp')
- residual_out: bfloat16 [64, 896, 8192], P('dp', 'tensor')
All inputs are finite; a program needn't handle non-finite values.
Results may differ from a plain program's by a relative error of at most 0.0051.
Values may be sent and summed in bfloat16 or wider, within the bound.
A program may use at most 192 MiB of HBM per device.

v0:
```python
import jax
import jax.numpy as jnp
from jax import lax
from jax.sharding import PartitionSpec as P

RANK = 32
REPLICAS = 2


def row_inner(left, right, precision):
    return lax.dot_general(
        left,
        right,
        (((0,), (0,)), ((), ())),
        precision=precision,
        preferred_element_type=jnp.float32,
    )


def orthonormal(p_rows, gram_matrix):
    factor = jnp.linalg.cholesky(gram_matrix)
    return lax.linalg.triangular_solve(
        factor, p_rows, left_side=False, lower=True, transpose_a=True
    )


def on_device(hidden_acts, out_grads, residual_in, q_prev):
    highest = lax.Precision.HIGHEST
    pieces = lax.axis_size("dp") // REPLICAS
    position = lax.axis_index("dp")
    replica = position // pieces
    piece_index = position % pieces
    tokens_each = hidden_acts.shape[1]
    rows_here = hidden_acts.shape[2]
    tensor_count = lax.axis_size("tensor")
    full_width = lax.all_gather(out_grads, "tensor", axis=1, tiled=True)
    every_token = lax.all_gather(full_width, "dp", axis=0, tiled=True)
    split_cols = every_token.reshape(tokens_each, tensor_count, REPLICAS, -1)
    own_grads = lax.dynamic_index_in_dim(split_cols, replica, 2, keepdims=False).reshape(
        tokens_each, -1
    )
    gradient = row_inner(hidden_acts[0], own_grads, None)
    merged = (gradient + residual_in[0].astype(jnp.float32)).astype(jnp.bfloat16)
    p_local = jnp.dot(merged, q_prev, preferred_element_type=jnp.float32)
    block_rows = pieces * rows_here
    every_piece = lax.all_gather(p_local, "dp", axis=0, tiled=True)
    p_block = every_piece.reshape(REPLICAS, block_rows, RANK).sum(axis=0)
    gram_matrix = lax.psum(row_inner(p_block, p_block, highest), "tensor")
    p_basis = orthonormal(p_block, gram_matrix)
    p_low = p_basis.astype(jnp.bfloat16)
    p_mine = lax.dynamic_slice_in_dim(p_low, piece_index * rows_here, rows_here, 0)
    column_count = merged.shape[1] // lax.axis_size("dp")
    q_full = lax.psum(row_inner(merged, p_mine, None), ("dp", "tensor")) / REPLICAS
    q_part = lax.dynamic_slice_in_dim(q_full, position * column_count, column_count, 0)
    q_low = q_full.astype(jnp.bfloat16)
    approx = jnp.dot(p_mine, q_low.T, preferred_element_type=jnp.float32)
    residual_out = (merged.astype(jnp.float32) - approx)[None].astype(jnp.bfloat16)
    return (p_basis, q_part, residual_out)


def solution(mesh):
    in_specs = (P("dp", None, "tensor"), P("dp", "tensor"), P("dp", "tensor", None), P())
    out_specs = (P("tensor", None), P("dp", None), P("dp", "tensor", None))
    return jax.shard_map(
        on_device, mesh=mesh, in_specs=in_specs, out_specs=out_specs, check_vma=False
    )
```

profile of v0, /device:TPU:1, one launch (start us, length us, event | category | flops | bytes accessed | tf_op | source)
XLA Modules:
  0.0 689.1 jit_solution(17416579119321483750)
XLA Ops:
  7.2 13.4 %all_gather.9 = bf16[12,16384]{1,0:T(8,128)(2,1)} all-gather(bf16[12,4096]{1,0:T(8,128)(2,1)} %param.5), channel_id=1, replica_groups=mesh['dp'=64,'tensor'=4] {'tensor'}, dimensions={1}, use_global_device_ids=true | all-gather | bytes 491520 | tf_op jit(solution)/shard_map/all_gather | solution.py:36
  20.8 147.0 %all-gather.5.cloned.1.call-done = bf16[64,12,16384]{2,1,0:T(8,128)(2,1)} async-done(((bf16[1,12,16384]{2,1,0:T(8,128)(2,1)}), bf16[64,12,16384]{2,1,0:T(8,128)(2,1)}) %all-gather.5.cloned.1.call-update) | async-done | bytes 25165840 | tf_op jit(solution)/shard_map/all_gather | solution.py:37
  167.8 36.5 %reshape.28 = bf16[768,4,2,2048]{3,2,1,0:T(2,128)(2,1)} reshape(bf16[64,12,16384]{2,1,0:T(8,128)(2,1)} %all-gather.5.cloned.1.call-done) | data formatting | bytes 50331648 | tf_op jit(solution)/shard_map/reshape | solution.py:38
  204.3 32.1 %constant_dynamic-slice_fusion.1 = bf16[768,4,1,2048]{3,2,1,0:T(2,128)(2,1)} fusion(bf16[768,4,2,2048]{3,2,1,0:T(2,128)(2,1)} %reshape.28, s32[]{:T(128)S(6)} %select_n.26), kind=kLoop, calls=%fused_computation.25 | loop fusion | bytes 25165828 | tf_op jit(solution)/shard_map/jit(dynamic_index_in_dim)/dynamic_slice | solution.py:39
  236.4 57.8 %copy.13 = bf16[768,4,1,2048]{0,3,1,2:T(8,128)(2,1)} copy(bf16[768,4,1,2048]{3,2,1,0:T(2,128)(2,1)} %constant_dynamic-slice_fusion.1) | data formatting | bytes 25165824 | tf_op jit(solution)/shard_map/jit(dynamic_index_in_dim)/dynamic_slice | solution.py:39
  294.2 13.3 %fusion.2 = bf16[224,8192]{1,0:T(8,128)(2,1)S(1)} fusion(bf16[768,8192]{0,1:T(8,128)(2,1)} %bitcast.36, bf16[1,224,8192]{2,1,0:T(8,128)(2,1)} %param.6, bf16[1,768,224]{1,2,0:T(8,128)(2,1)S(1)} %copy-done.3), kind=kOutput, calls=%fused_computation.4 | convolution fusion | flops 2824077312 | bytes 20267008 | tf_op jit(solution)/shard_map/dot_general | solution.py:11
  307.4 1.8 copy-done.1
  309.3 1.8 convolution_bitcast_fusion.1
  311.2 74.3 %all-gather.7.cloned.1.call-done = f32[64,224,32]{1,2,0:T(8,128)} async-done(((f32[1,224,32]{1,2,0:T(8,128)}), f32[64,224,32]{1,2,0:T(8,128)}) %all-gather.7.cloned.1.call-update) | async-done | bytes 1835024 | tf_op jit(solution)/shard_map/all_gather | solution.py:46
  385.5 2.8 copy.14
  388.3 3.5 reshape.30
  391.8 3.7 reduce_sum.9
  395.5 0.9 fusion.13
  396.3 13.1 %psum.14 = f32[32,32]{0,1:T(8,128)S(1)} all-reduce(f32[32,32]{0,1:T(8,128)S(1)} %fusion.13), channel_id=1, replica_groups=mesh['dp'=64,'tensor'=4] {'tensor'}, use_global_device_ids=true, to_apply=%region_1.2 | all-reduce | flops 1024 | bytes 8192 | tf_op jit(solution)/shard_map/psum | solution.py:48
  409.6 2.9 cholesky.16
  412.5 0.6 compare_reduce_fusion
  413.2 0.7 fusion.6
  413.8 2.4 custom-call.6
  416.3 0.9 fusion.7
  417.2 4.2 fusion.10
  421.5 253.7 %all-reduce.2.cloned.1.call-done = f32[8192,32]{0,1:T(8,128)} async-done(((f32[8192,32]{0,1:T(8,128)}), f32[8192,32]{0,1:T(8,128)}) %all-reduce.2.cloned.1.call-update) | async-done | bytes 1048592 | tf_op jit(solution)/shard_map/psum | solution.py:53
  675.2 1.3 broadcast_multiply_fusion
  676.5 0.6 constant_dynamic-slice_fusion
  677.1 5.4 fusion.3
  (16 shorter events, 0.3 us)
Async XLA Ops:
  7.2 302.1 %copy-start = (bf16[8192,32]{0,1:T(8,128)(2,1)S(1)}, bf16[8192,32]{0,1:T(8,128)(2,1)}, u32[]{:S(2)}) copy-start(bf16[8192,32]{0,1:T(8,128)(2,1)} %param.7) | copy-start | bytes 1572868
  7.2 160.6 %all-gather.5.cloned.1.call-start = ((), (), s32[]{:S(2)}) async-start(), calls=%async_computation.1 | async-start | bytes 34078720 | tf_op jit(solution)/shard_map/all_gather | solution.py:37
  20.7 364.8 %all-gather.7.cloned.1.call-start = ((), (), s32[]{:S(2)}) async-start(), calls=%async_computation.2 | async-start | bytes 2129920 | tf_op jit(solution)/shard_map/all_gather | solution.py:46
  236.4 57.8 %copy-start.3 = (bf16[1,768,224]{1,2,0:T(8,128)(2,1)S(1)}, bf16[1,768,224]{1,2,0:T(8,128)(2,1)}, u32[]{:S(2)}) copy-start(bf16[1,768,224]{1,2,0:T(8,128)(2,1)} %param.4) | copy-start | bytes 1032196
  307.4 1.8 copy-start.1
  311.1 364.1 %all-reduce.2.cloned.1.call-start = ((), (), s32[]{:S(2)}) async-start(), calls=%async_computation | async-start | bytes 2097152 | tf_op jit(solution)/shard_map/psum | solution.py:53
  417.2 259.9 %copy-start.2 = (f32[7168,32]{0,1:T(8,128)}, f32[7168,32]{0,1:T(8,128)S(1)}, u32[]{:S(2)}) copy-start(f32[7168,32]{0,1:T(8,128)S(1)} %fusion.7) | copy-start | bytes 2752516
Sparse Core Ops, SparseCore 0:
  20.8 146.9 all-gather.4
  311.3 74.1 all-gather.6
  421.6 253.5 all-reduce.1
where the time goes:
time: 692 us; the launch traced here: 689 us
  waiting for transfers between devices  475 us (69%)
  local copies, waits for them, and re-layouts  135 us (20%)
  blocking collectives  26.6 us (4%)
  matrix products  26.5 us (4%)
  between operations  13.9 us (2%)
  other arithmetic  11.7 us (2%)
    psum x1, waiting for transfers between devices, on_device(): lax.psum(row_inner(merged, p_mine, None), ('dp', 'tensor')) / REPLICAS  254 us
    all_gather x1, waiting for transfers between devices, on_device(): every_token = lax.all_gather(full_width, 'dp', axis=0, tiled=True)  147 us
    dynamic_slice x2, local copies, waits for them, and re-layouts, on_device(): lax.dynamic_index_in_dim(split_cols, replica, 2, keepdims=False)  89.8 us
    all_gather x1, waiting for transfers between devices, on_device(): every_piece = lax.all_gather(p_local, 'dp', axis=0, tiled=True)  74.3 us
    reshape x1, local copies, waits for them, and re-layouts, on_device(): split_cols = every_token.reshape(tokens_each, tensor_count, REPLICAS, -1)  36.5 us
    dot_general x3, matrix products, row_inner(): lax.dot_general(left, right, (((0,), (0,)), ((), ())), precision=precisio...  18.3 us
  transfers between devices with their start and end apart: 3, of which 3 were waited for; matrix products, arithmetic and copies ran while one was open for 0% of the time, Pallas kernels for 0%

commit v1 on v0

v1 whole, which is shorter than its diff:
```python
import jax
import jax.numpy as jnp
from jax import lax
from jax.experimental import pallas as pl
from jax.experimental.pallas import tpu as pltpu
from jax.sharding import PartitionSpec as P

NZ, NX, NC, NY = 8, 4, 2, 4
RANK = 32
TOK, TOK_DEV = 768, 12
ROWS = 224
D = 8192
PAD = 256
NQ = 4
DEEP = 2
F32, BF16 = jnp.float32, jnp.bfloat16
HIGH = lax.Precision.HIGHEST
MESH = pl.DeviceIdType.MESH


def link_of(h, axis, step):
    return 2 * ((axis + h) % 2) + (0 if step == 1 else 1)


def plan():
    hop, lat, core_lat, work = 2.1, 2.8, 1.6, 0.65
    now, count, order, arrivals = 0.0, 0, [], []
    parts, both = {}, {}
    queue, done, free = [[] for _ in range(4)], [[] for _ in range(4)], [0.0] * 4
    starts = [(4.6 + 2.1 * h, h) for h in range(NQ)]
    todo = [(h, rel) for h in range(NQ) for rel in (0, 3, 1, 2)]

    def put(kind, size, key, push):
        nonlocal count
        count += 1
        queue[link_of(push[0], push[4], push[5])].append(((kind, push[0], count), size, key, push))

    def spread(h, f):
        put(2, 1.0, (h, f, 3), (h, f, 0, None, 1, 1))
        put(2, 1.0, (h, f, 1), (h, f, 0, None, 1, -1))

    while len(order) < NQ * 40:
        arrivals.sort()
        if starts and starts[0][0] <= now:
            h = starts.pop(0)[1]
            order.append(("begin", h))
            now += 0.3
            put(0, 1.0, (h, 3, 0), (h, 0, 0, None, 0, 1))
            put(0, 1.0, (h, 1, 0), (h, 0, 0, None, 0, -1))
            spread(h, 0)
            both[h, 0, 0] = now + core_lat
            continue
        if arrivals and arrivals[0][0] <= now:
            h, f, s = arrivals.pop(0)[1]
            if f == 2 and s == 0 or s == 2:
                parts[h, f, s] = parts.get((h, f, s), 0) + 1
                if parts[h, f, s] < 2:
                    continue
            order.append(("forward", h, f, s))
            if s == 0:
                if f != 2:
                    step = 1 if f == 3 else -1
                    put(1, 0.5, (h, 2, 0), (h, f, 0, 0 if f == 3 else 1, 0, step))
                spread(h, f)
            elif s != 2:
                step = 1 if s == 3 else -1
                put(3, 0.5, (h, f, 2), (h, f, s, 0 if s == 3 else 1, 1, step))
            both[h, f, s] = now + core_lat
            now += 0.08
            continue
        sent = False
        for link in range(4):
            if queue[link] and (len(done[link]) < DEEP or done[link][-DEEP] <= now):
                queue[link].sort()
                _, size, key, push = queue[link].pop(0)
                free[link] = max(now, free[link]) + size * hop
                done[link].append(free[link])
                arrivals.append((free[link] + lat, key))
                order.append(("push",) + push)
                now += 0.04
                sent = True
                break
        if sent:
            continue
        ready = None
        for h, rel in todo:
            need = [(h, i, rel) if h % 2 == 0 else (h, rel, i) for i in range(4)]
            if all(both.get(k, 1e9) <= now for k in need):
                ready = (h, rel)
                break
        if ready:
            todo.remove(ready)
            order.append(("compute",) + ready)
            now += work
            continue
        times = [t for t, _ in arrivals[:1]] + [t for t, _ in starts[:1]]
        times += [t for t in both.values() if t > now]
        times += [
            done[link][-DEEP] for link in range(4)
            if queue[link] and len(done[link]) >= DEEP and done[link][-DEEP] > now
        ]
        now = max(now + 1e-3, min(times))
    return order


ORDER = plan()


def iota(shape, axis):
    return lax.broadcasted_iota(jnp.int32, shape, axis)


def div12(v):
    return (v * 5462) >> 16


def one_hot(cond):
    return jnp.where(cond, 1.0, 0.0).astype(BF16)


def dot(a, b, dims=((1,), (0,)), precision=None):
    return lax.dot_general(
        a, b, (dims, ((), ())), precision=precision, preferred_element_type=F32
    )


def eliminate(gram):
    row, lane = iota((RANK, 128), 0), iota((RANK, 128), 1)
    work = gram + jnp.where(lane == row + RANK, 1.0, 0.0)
    for k in range(RANK):
        column = jnp.broadcast_to(work[:, k:k + 1], (RANK, 128))
        scale = lax.rsqrt(column[k:k + 1, :])
        pivot_row = work[k:k + 1, :] * scale
        below = work - (column * scale) * pivot_row
        work = jnp.where(row > k, below, jnp.where(row == k, pivot_row, work))
    inverse = pltpu.roll(work, 128 - RANK, 1)
    return jnp.where(lane < RANK, inverse, 0.0)


def main_kernel(
    hid_hbm, og_hbm, q_hbm, res_hbm,
    mer_out, pb_out, qt_out, low_out,
    hid, og, pack, zbuf, grads, hid_t, res, mer, qv, pacc, pt_mine, pt_other, pg, pb, low,
    wb, wr, c2r, w2, c3r, gram_c, gram_p, gram_z, zw, qt,
    z_send, z_sem, link_send, xy_sem, core_send, core_sem, sends, b_sem, gc_sem, c1_sem,
    gp_sem, c2_sem, c3_sem, gz_sem, zw_sem, pz_sem, px_sem, pc_sem, ag_sem, agc_sem,
    local_sem, out_sem,
):
    dp, y = lax.axis_index("dp"), lax.axis_index("tensor")
    z, x, c = dp // 8, (dp // 2) % 4, dp % 2
    other = 1 - c
    replica = z // 4

    def device(dz=0, dx=0, dc=0, dy=0):
        return (((z + dz) % NZ) * 8 + ((x + dx) % NX) * 2 + (c + dc) % NC, (y + dy) % NY)

    sibling = device(dc=1)

    def remote(src, dst, send_sem, recv_sem, there):
        return pltpu.make_async_remote_copy(
            src_ref=src, dst_ref=dst, send_sem=send_sem, recv_sem=recv_sem,
            device_id=there, device_id_type=MESH,
        )

    def send(src, dst, send_sem, recv_sem, there):
        copy = remote(src, dst, send_sem, recv_sem, there)
        copy.start()
        return copy

    def arrived(ref, sem):
        remote(ref, ref, core_send.at[0], sem, sibling).wait_recv()

    def left(ref, sem):
        remote(ref, ref, sem, b_sem.at[0], sibling).wait_send()

    pending = []

    def later(ref, number):
        pending.append((ref, sends.at[number]))

    barrier = pltpu.get_barrier_semaphore()
    partners = [device(dz=d) for d in range(1, NZ)] + [sibling]
    partners += [
        device(dx=dx, dy=dy) for dx in range(NX) for dy in range(NY) if (dx, dy) != (0, 0)
    ]
    for partner in partners:
        pl.semaphore_signal(barrier, inc=1, device_id=partner, device_id_type=MESH)

    og_copy = pltpu.make_async_copy(og_hbm, og, local_sem.at[0])
    hid_copy = pltpu.make_async_copy(hid_hbm, hid, local_sem.at[1])
    q_copy = pltpu.make_async_copy(q_hbm, qv, local_sem.at[2])
    res_copy = pltpu.make_async_copy(res_hbm, res, local_sem.at[3])
    for copy in (og_copy, hid_copy, q_copy, res_copy):
        copy.start()

    og_copy.wait()
    total = jnp.zeros((48, 1024), F32)
    for g in range(4):
        pick = one_hot(iota((48, TOK_DEV), 0) == iota((48, TOK_DEV), 1) + g * TOK_DEV)
        lanes = [og[:, i * 512 + g * 128:i * 512 + (g + 1) * 128] for i in range(8)]
        total += dot(pick, jnp.concatenate(lanes, axis=1))
    for i in range(8):
        pack[i] = total[:, i * 128:(i + 1) * 128].astype(BF16)
    for h in range(NQ):
        zbuf[h * NZ + z] = pack[replica * NQ + h]

    pl.semaphore_wait(barrier, len(partners))

    def send_z(h):
        if h:
            left(zbuf.at[pl.ds(0, 7)], z_send.at[h - 1])
        for d in range(1, NZ):
            there = (z + d) % NZ // 4
            send(
                pack.at[there * NQ + h], zbuf.at[h * NZ + z], z_send.at[h], z_sem.at[h],
                device(dz=d),
            )

    send_z(0)

    hid_copy.wait()
    hidden = hid[...]
    for i in range(3):
        r = iota((1, 256), 1) + i * 256
        rx = jnp.where(r >= 192, 1, 0) + jnp.where(r >= 384, 1, 0) + jnp.where(r >= 576, 1, 0)
        r = r - rx * 192
        rc = jnp.where(r >= 96, 1, 0)
        r = r - rc * 96
        rz = div12(r)
        token = rz * 96 + rx * 24 + rc * 12 + (r - rz * 12)
        pick = one_hot(iota((TOK, 256), 0) == token)
        hid_t[:, i * 256:(i + 1) * 256] = dot(hidden, pick).astype(BF16)
    send_z(1)
    pacc[...] = jnp.zeros_like(pacc)
    res_copy.wait()
    q_copy.wait()

    def block(h, first, second, part=None, core=None):
        dx, dy = (first, second) if h % 2 == 0 else (second, first)
        row = (x + dx) % NX * 192 + (c if core is None else core) * 96
        count = 96
        if part is not None:
            row, count = row + 48 * part, 48
        return grads.at[(y + dy) % NY * NQ + h, pl.ds(pl.multiple_of(row, 16), count)]

    flights = [[] for _ in range(4)]

    def push(h, first, second, part, axis, step):
        link = link_of(h, axis, step)
        number = len(flights[link])
        if number >= DEEP:
            flights[link][number - DEEP].wait_send()
        there = device(dx=step) if link < 2 else device(dy=step)
        f, s = first, second
        if axis == 0:
            f = (first - step) % 4
        else:
            s = (second - step) % 4
        ref = block(h, first, second, part)
        flights[link].append(
            send(ref, ref, link_send.at[link, number % DEEP], xy_sem.at[h, f * 4 + s], there)
        )

    def share(h, first, second):
        ref = block(h, first, second)
        rel = second if h % 2 == 0 else first
        send(ref, ref, core_send.at[0], core_sem.at[h, rel], sibling)

    def begin(h):
        if h + 2 < NQ:
            send_z(h + 2)
        arrived(zbuf.at[pl.ds(0, 7)], z_sem.at[h])
        packed = zbuf[h * NZ:(h + 1) * NZ].reshape(384, 128)
        row = pl.multiple_of(x * 192 + c * 96, 16)
        for g in range(4):
            r, s = iota((96, 384), 0), iota((96, 384), 1)
            pick = one_hot(s == r + div12(r) * 36 + g * TOK_DEV)
            grads[y * NQ + h, pl.ds(row, 96), g * 128:(g + 1) * 128] = dot(pick, packed).astype(BF16)
        share(h, 0, 0)

    def forward(h, f, s):
        arrived(block(h, f, s), xy_sem.at[h, f * 4 + s])
        share(h, f, s)

    blocks_out = []

    def add_left(cols):
        pacc[...] += dot(qv[:, cols], mer[:, cols], ((1,), (1,)))

    def compute(h, rel):
        arrived(grads.at[0, pl.ds(0, 384)], core_sem.at[h, rel])
        yb = (y + rel) % NY
        base = pl.multiple_of(yb * 2048 + h * 512, 512)

        def tile(i, carry):
            col = pl.multiple_of(base + i * 256, 256)
            part = grads[yb * NQ + h, :, pl.ds(pl.multiple_of(i * 256, 256), 256)]
            merged = dot(hid_t[...], part) + res[:, pl.ds(col, 256)].astype(F32)
            mer[:, pl.ds(col, 256)] = merged.astype(BF16)
            return carry

        if blocks_out:
            add_left(blocks_out[-1])
        lax.fori_loop(0, 2, tile, 0, unroll=True)
        cols = pl.ds(base, 512)
        pltpu.make_async_copy(mer.at[:, cols], mer_out.at[:, cols], out_sem.at[0]).start()
        blocks_out.append(cols)

    steps = {"begin": begin, "forward": forward, "compute": compute, "push": push}
    for what, *where in ORDER:
        steps[what](*where)

    def end():
        for ref, sem in pending:
            left(ref, sem)
        left(zbuf.at[pl.ds(0, 7)], z_send.at[NQ - 1])
        for link in range(4):
            for copy in flights[link][-DEEP:]:
                copy.wait_send()
        left(grads.at[pl.ds(0, 8)], core_send.at[0])
        pltpu.make_async_copy(mer, mer_out, out_sem.at[0]).wait()

    add_left(blocks_out[-1])
    pt_mine[...] = jnp.zeros_like(pt_mine)
    pt_mine[:, 0:ROWS] = pacc[...]
    send(pt_mine, pt_other, sends.at[0], b_sem.at[0], device(dz=4))
    later(pt_mine, 0)
    arrived(pt_other, b_sem.at[0])
    pt = pt_mine[...] + pt_other[...]
    slot = c * 16 + z % 4 * 4 + x
    pg[slot] = pt

    gram = dot(pt, jnp.concatenate([pt, jnp.zeros((96, PAD), F32)], axis=0), ((1,), (1,)), HIGH)
    packed = gram[0:8]
    for g in range(1, 4):
        packed += pltpu.roll(gram[8 * g:8 * g + 8], 32 * g, 1)
    gram_c[0] = packed
    send(gram_c.at[0], gram_c.at[1], sends.at[1], gc_sem.at[0], sibling)
    later(gram_c.at[0], 1)
    for d in range(1, 4):
        send(pg.at[slot], pg.at[slot], sends.at[3], px_sem.at[0], device(dx=d))
    later(pg.at[pl.ds(0, 3)], 3)

    hi = pt.astype(BF16)
    rest = pt - hi.astype(F32)
    mid = rest.astype(BF16)
    rest = (rest - mid.astype(F32)).astype(BF16)
    terms = jnp.concatenate([hi, mid, rest], axis=0)[:, :ROWS]

    def w_tiles(first):
        def tile(i, carry):
            nb = first + i * 2
            col = pl.multiple_of(nb * 128, 256)
            product = dot(terms, mer[:, pl.ds(col, 256)])
            total = product[0:32] + (product[32:64] + product[64:96])
            wb[nb] = total[:, 0:128]
            wb[nb + 1] = total[:, 128:256]
            return carry

        lax.fori_loop(0, 8, tile, 0, unroll=4)

    for h in range(2):
        w_tiles(other * 32 + h * 16)
        send(
            wb.at[pl.ds(other * 32 + h * 16, 16)], wr.at[pl.ds(h * 16, 16)],
            sends.at[2], c1_sem.at[h], sibling,
        )
        if h:
            continue
        arrived(gram_c.at[0], gc_sem.at[0])
        spot = x * 4 + y
        gram_p[spot] = gram_c[0] + gram_c[1]
        for dx in range(NX):
            for dy in range(NY):
                if (dx, dy) != (0, 0):
                    send(
                        gram_p.at[spot], gram_p.at[spot], sends.at[4], gp_sem.at[0],
                        device(dx=dx, dy=dy),
                    )
        later(gram_p.at[pl.ds(0, 15)], 4)
    later(wr, 2)
    places = (x, y)

    for h in range(2):
        w_tiles(c * 32 + h * 16)
        arrived(wr.at[pl.ds(h * 16, 16)], c1_sem.at[h])
        at = pl.ds(c * 32 + h * 16, 16)
        wb[at] = wb[at] + wr[pl.ds(h * 16, 16)]
        for d in range(1, 4):
            there = (places[h] + d) % 4
            send(
                wb.at[pl.ds(c * 32 + h * 16 + there * 4, 4)], c2r.at[h * 4 + places[h]],
                sends.at[5], c2_sem.at[h], device(dx=d) if h == 0 else device(dy=d),
            )
    later(c2r.at[pl.ds(0, 6)], 5)

    arrived(gram_p.at[pl.ds(0, 15)], gp_sem.at[0])
    total = gram_p[0]
    for i in range(1, 16):
        total += gram_p[i]
    gram_z[z] = total
    for d in range(1, NZ):
        send(gram_z.at[z], gram_z.at[z], sends.at[9], gz_sem.at[0], device(dz=d))
    later(gram_z.at[pl.ds(0, 7)], 9)

    arrived(pg.at[pl.ds(0, 3)], px_sem.at[0])
    group = pg.at[pl.ds(c * 16 + z % 4 * 4, 4)]
    for d in (1, -1, 2):
        send(group, group, sends.at[8], pz_sem.at[0], device(dz=d))
    later(pg.at[pl.ds(0, 12)], 8)

    for h in range(2):
        arrived(c2r.at[pl.ds(0, 3)], c2_sem.at[h])
        total = wb[pl.ds(c * 32 + h * 16 + places[h] * 4, 4)]
        for d in range(1, 4):
            total += c2r[h * 4 + (places[h] + d) % 4]
        w2[h] = total
        for d in range(1, 4):
            there = (places[1 - h] + d) % 4
            send(
                w2.at[h, there], c3r.at[h * 4 + places[1 - h]],
                sends.at[7], c3_sem.at[h], device(dy=d) if h == 0 else device(dx=d),
            )
    later(c3r.at[pl.ds(0, 6)], 7)

    arrived(gram_z.at[pl.ds(0, 7)], gz_sem.at[0])
    total = gram_z[0]
    for i in range(1, NZ):
        total += gram_z[i]
    total = total * 0.5
    lane = iota((RANK, 128), 1)
    gram = jnp.concatenate(
        [total] + [pltpu.roll(total, 128 - 32 * g, 1) for g in range(1, 4)], axis=0
    )
    inverse = eliminate(jnp.where(lane < RANK, gram, 0.0))[:, 0:RANK]

    for h in range(2):
        arrived(c3r.at[pl.ds(0, 3)], c3_sem.at[h])
        total = w2[h, places[1 - h]]
        for d in range(1, 4):
            total += c3r[h * 4 + (places[1 - h] + d) % 4]
        zw[h * NZ + z] = (dot(inverse, total, precision=HIGH) * 0.5).astype(BF16)
        for d in range(1, NZ):
            send(zw.at[h * NZ + z], zw.at[h * NZ + z], sends.at[10], zw_sem.at[h], device(dz=d))
    later(zw.at[pl.ds(0, 14)], 10)

    mine = c * 16 + x * 4 + y
    for h in range(2):
        arrived(zw.at[pl.ds(0, 7)], zw_sem.at[h])
        total = zw[h * NZ].astype(F32)
        for i in range(1, NZ):
            total += zw[h * NZ + i].astype(F32)
        qt[h, mine] = total.astype(BF16)
        for dx in range(NX):
            for dy in range(NY):
                if (dx, dy) != (0, 0):
                    send(
                        qt.at[h, mine], qt.at[h, mine], sends.at[11 + h],
                        ag_sem.at[h * dx + h], device(dx=dx, dy=dy),
                    )
        later(qt.at[h, pl.ds(0, 15)], 11 + h)

    arrived(pg.at[pl.ds(0, 12)], pz_sem.at[0])
    half = pg.at[pl.ds(c * 16, 16)]
    send(half, half, sends.at[14], pc_sem.at[0], sibling)
    later(half, 14)
    own = dot(inverse, pg[slot], precision=HIGH)
    own = jnp.concatenate([own, jnp.zeros((96, PAD), F32)], axis=0).T
    low[...] = own[0:ROWS].astype(BF16)
    low_copy = pltpu.make_async_copy(low, low_out, local_sem.at[0])
    low_copy.start()
    arrived(half, pc_sem.at[0])
    for i in range(8):
        blocks = []
        for p in range(4 * i, 4 * i + 4):
            blocks.append(pg[p % 2 * 16 + p // 8 * 4 + p // 2 % 4][:, 0:ROWS])
        blocks = jnp.concatenate(blocks, axis=1)
        pb[:, i * 896:(i + 1) * 896] = dot(inverse, blocks, precision=HIGH)
    pb_copy = pltpu.make_async_copy(pb, pb_out, local_sem.at[1])
    pb_copy.start()

    arrived(qt.at[0, pl.ds(0, 15)], ag_sem.at[0])
    ours = qt.at[0, pl.ds(c * 16, 16)]
    send(ours, ours, sends.at[13], agc_sem.at[0], sibling)
    for dx in (0, 1, 3, 2):
        rows = qt.at[1, pl.ds(c * 16 + (x + 4 - dx) % 4 * 4, 4)]
        arrived(qt.at[1, pl.ds(0, 4 if dx else 3)], ag_sem.at[1 + dx])
        send(rows, rows, sends.at[13], agc_sem.at[0], sibling)
    later(qt.at[0], 13)
    arrived(qt.at[0], agc_sem.at[0])
    qt_copy = pltpu.make_async_copy(qt, qt_out, local_sem.at[2])
    qt_copy.start()
    end()
    low_copy.wait()
    pb_copy.wait()
    qt_copy.wait()


def exchange(
    hidden, out_grads, q_prev, residual,
):
    dma = pltpu.SemaphoreType.DMA
    any_spec = pl.BlockSpec(memory_space=pl.ANY)
    return pl.pallas_call(
        main_kernel,
        out_shape=(
            jax.ShapeDtypeStruct((ROWS, D), BF16),
            jax.ShapeDtypeStruct((RANK, 32 * ROWS), F32),
            jax.ShapeDtypeStruct((2, 32, RANK, 128), BF16),
            jax.ShapeDtypeStruct((ROWS, 128), BF16),
        ),
        in_specs=[any_spec] * 4,
        out_specs=(any_spec,) * 4,
        scratch_shapes=[
            pltpu.VMEM((ROWS, TOK), BF16),
            pltpu.VMEM((TOK_DEV, 4096), BF16),
            pltpu.VMEM((8, 48, 128), BF16),
            pltpu.VMEM((NQ * NZ, 48, 128), BF16),
            pltpu.VMEM((4 * NQ, TOK, 512), BF16),
            pltpu.VMEM((ROWS, TOK), BF16),
            pltpu.VMEM((ROWS, D), BF16),
            pltpu.VMEM((ROWS, D), BF16),
            pltpu.VMEM((RANK, D), BF16),
            pltpu.VMEM((RANK, ROWS), F32),
            pltpu.VMEM((RANK, PAD), F32),
            pltpu.VMEM((RANK, PAD), F32),
            pltpu.VMEM((32, RANK, PAD), F32),
            pltpu.VMEM((RANK, 32 * ROWS), F32),
            pltpu.VMEM((ROWS, 128), BF16),
            pltpu.VMEM((64, RANK, 128), F32),
            pltpu.VMEM((32, RANK, 128), F32),
            pltpu.VMEM((8, 4, RANK, 128), F32),
            pltpu.VMEM((2, 4, RANK, 128), F32),
            pltpu.VMEM((8, RANK, 128), F32),
            pltpu.VMEM((2, 8, 128), F32),
            pltpu.VMEM((16, 8, 128), F32),
            pltpu.VMEM((NZ, 8, 128), F32),
            pltpu.VMEM((2 * NZ, RANK, 128), BF16),
            pltpu.VMEM((2, 32, RANK, 128), BF16),
            dma((NQ,)),
            dma((NQ,)),
            dma((4, DEEP)),
            dma((NQ, 16)),
            dma((1,)),
            dma((NQ, 4)),
            dma((15,)),
            dma((1,)),
            dma((1,)),
            dma((2,)),
            dma((1,)),
            dma((2,)),
            dma((2,)),
            dma((1,)),
            dma((2,)),
            dma((1,)),
            dma((1,)),
            dma((1,)),
            dma((5,)),
            dma((1,)),
            dma((4,)),
            dma((1,)),
        ],
        name="exchange",
        compiler_params=pltpu.CompilerParams(
            collective_id=0, has_side_effects=True, vmem_limit_bytes=60 * 2**20
        ),
    )(hidden, out_grads, q_prev, residual)


def final_kernel(
    mer_hbm, pb_hbm, qt_hbm, low_hbm, res_hbm, p_hbm, q_hbm,
    mer, res, qt, low, q_new, pb, in_sem, out_sem,
):
    low_copy = pltpu.make_async_copy(low_hbm, low, in_sem.at[0])
    qt_copy = pltpu.make_async_copy(qt_hbm, qt, in_sem.at[1])
    p_copy = pltpu.make_async_copy(pb_hbm, pb, in_sem.at[2])
    low_copy.start()
    qt_copy.start()
    pieces = []
    for i in range(4):
        cols = pl.ds(i * 2048, 2048)
        pieces.append(pltpu.make_async_copy(mer_hbm.at[:, cols], mer.at[:, cols], in_sem.at[3 + i]))
        pieces[-1].start()
    p_copy.start()

    def place(nb):
        core, part, v = nb // 32, nb % 32 // 16, nb % 16
        return part, core * 16 + (v if part == 0 else v % 4 * 4 + v // 4)

    low_copy.wait()
    qt_copy.wait()
    p_low = low[:, 0:RANK]
    for i in range(4):
        pieces[i].wait()
        for nb in range(i * 16, i * 16 + 16, 2):
            q_low = jnp.concatenate([qt[place(nb)], qt[place(nb + 1)]], axis=1)
            cols = slice(nb * 128, nb * 128 + 256)
            res[:, cols] = (mer[:, cols].astype(F32) - dot(p_low, q_low)).astype(BF16)
        cols = pl.ds(i * 2048, 2048)
        pltpu.make_async_copy(res.at[:, cols], res_hbm.at[:, cols], out_sem.at[0]).start()
        if i == 0:
            p_copy.wait()
            p_copy = pltpu.make_async_copy(pb, p_hbm, in_sem.at[2])
            p_copy.start()

    nb = lax.axis_index("dp")
    part, v = nb % 32 // 16, nb % 16
    slot = nb // 32 * 16 + jnp.where(part == 0, v, v % 4 * 4 + v // 4)
    q_new[...] = qt[part, slot].astype(F32)
    q_copy = pltpu.make_async_copy(q_new, q_hbm, in_sem.at[0])
    q_copy.start()
    q_copy.wait()
    p_copy.wait()
    pltpu.make_async_copy(res, res_hbm, out_sem.at[0]).wait()


def finish(mer, pb, qt, low):
    any_spec = pl.BlockSpec(memory_space=pl.ANY)
    return pl.pallas_call(
        final_kernel,
        out_shape=(
            jax.ShapeDtypeStruct((ROWS, D), BF16),
            jax.ShapeDtypeStruct((RANK, 32 * ROWS), F32),
            jax.ShapeDtypeStruct((RANK, 128), F32),
        ),
        in_specs=[any_spec] * 4,
        out_specs=(any_spec,) * 3,
        scratch_shapes=[
            pltpu.VMEM((ROWS, D), BF16),
            pltpu.VMEM((ROWS, D), BF16),
            pltpu.VMEM((2, 32, RANK, 128), BF16),
            pltpu.VMEM((ROWS, 128), BF16),
            pltpu.VMEM((RANK, 128), F32),
            pltpu.VMEM((RANK, 32 * ROWS), F32),
            pltpu.SemaphoreType.DMA((7,)),
            pltpu.SemaphoreType.DMA((1,)),
        ],
        name="finish",
        compiler_params=pltpu.CompilerParams(vmem_limit_bytes=60 * 2**20),
    )(mer, pb, qt, low)


def on_device(hidden_acts, out_grads, residual_in, q_prev):
    parts = exchange(hidden_acts[0].T, out_grads, q_prev.T, residual_in[0])
    residual_out, p_basis, q_new = finish(*parts)
    return p_basis.T, q_new.T, residual_out[None]


def solution(mesh):
    in_specs = (P("dp", None, "tensor"), P("dp", "tensor"), P("dp", "tensor", None), P())
    out_specs = (P("tensor", None), P("dp", None), P("dp", "tensor", None))
    return jax.shard_map(
        on_device, mesh=mesh, in_specs=in_specs, out_specs=out_specs, check_vma=False
    )
```

time: 692 us -> 95.9 us (0.14)
  waiting for transfers between devices: 475 us -> 0 us
  local copies, waits for them, and re-layouts: 135 us -> 0 us
  Pallas kernels: 0 us -> 95.2 us
  blocking collectives: 26.6 us -> 0 us
  matrix products: 26.5 us -> 0 us
  between operations: 13.9 us -> 0.64 us
  other arithmetic: 11.7 us -> 0 us
    psum x1 -> x0, waiting for transfers between devices: 254 us -> none  [on_device(): lax.psum(row_inner(merged, p_mine, None), ('dp', 'tensor')) / REPLICAS]
    all_gather x2 -> x0, waiting for transfers between devices: 221 us -> none  [the longest x1 147 us: on_device(): every_token = lax.all_gather(full_width, 'dp', axis=0, tiled=True)]
    pallas_call x0 -> x2, Pallas kernels: none -> 95.2 us  [the longest x1 90.6 us: exchange(): pl.pallas_call(main_kernel, out_shape=(jax.ShapeDtypeStruct((ROWS, D), BF...]
    dynamic_slice x3 -> x0, local copies, waits for them, and re-layouts: 90.5 us -> none  [the longest x2 89.8 us: on_device(): lax.dynamic_index_in_dim(split_cols, replica, 2, keepdims=False)]
    reshape x2 -> x0, local copies, waits for them, and re-layouts: 40.1 us -> none  [the longest x1 36.5 us: on_device(): split_cols = every_token.reshape(tokens_each, tensor_count, REPLICAS, -1)]
    dot_general x5 -> x0, matrix products: 25.6 us -> none  [the longest x3 18.3 us: row_inner(): lax.dot_general(left, right, (((0,), (0,)), ((), ())), precision=precisio...]
    all_gather x1 -> x0, blocking collectives: 13.4 us -> none  [on_device(): full_width = lax.all_gather(out_grads, 'tensor', axis=1, tiled=True)]
    psum x1 -> x0, blocking collectives: 13.1 us -> none  [on_device(): gram_matrix = lax.psum(row_inner(p_block, p_block, highest), 'tensor')]
  transfers between devices with their start and end apart: 3 -> 0, of which waited for: 3 -> 0; matrix products, arithmetic and copies ran while one was open for 0% -> 0% of each run, Pallas kernels for 0% -> 0%
where the time goes in v1:
time: 95.9 us; the launch traced here: 95.8 us
  Pallas kernels  95.2 us (99%)
    pallas_call x1, Pallas kernels, exchange(): pl.pallas_call(main_kernel, out_shape=(jax.ShapeDtypeStruct((ROWS, D), BF...  90.6 us
    pallas_call x1, Pallas kernels, finish(): pl.pallas_call(final_kernel, out_shape=(jax.ShapeDtypeStruct((ROWS, D), B...  4.59 us

profile of v1, /device:TPU:1, one launch (start us, length us, event | category | flops | bytes accessed | tf_op | source)
XLA Modules:
  0.0 95.8 jit_solution(13888993987337449202)
XLA Ops:
  0.6 90.6 %exchange.1 = (bf16[224,8192]{1,0:T(8,128)(2,1)}, f32[32,7168]{1,0:T(8,128)}, bf16[2,32,32,128]{3,2,1,0:T(8,128)(2,1)}, bf16[224,128]{1,0:T(8,128)(2,1)}) custom-call(bf16[224,768]{1,0:T(8,128)(2,1)} %bitcast.10, bf16[12,4096]{1,0:T(8,128)(2,1)} %og_hbm.1, bf16[32,8192]{1,0:T(8,128)(2,1)} %bitcast.9, bf16[224,8192]{1,0:T(8,128)(2,1)} %bitcast.8), custom_call_target="tpu_custom_call" | custom-call | tf_op jit(solution)/shard_map/exchange/pallas_call | solution.py:504
  91.2 4.6 %finish.1 = (bf16[224,8192]{1,0:T(8,128)(2,1)}, f32[32,7168]{1,0:T(8,128)}, f32[32,128]{1,0:T(8,128)}) custom-call(bf16[224,8192]{1,0:T(8,128)(2,1)} %get-tuple-element.10.mer_hbm, f32[32,7168]{1,0:T(8,128)} %get-tuple-element.11.pb_hbm, bf16[2,32,32,128]{3,2,1,0:T(8,128)(2,1)} %get-tuple-element.12.qt_hbm, bf16[224,128]{1,0:T(8,128)(2,1)} %get-tuple-element.13.low_hbm), custom_call_target="tpu_custom_call" | custom-call | tf_op jit(solution)/shard_map/finish/pallas_call | solution.py:619

commit v2 on v1

--- a/solution.py
+++ b/solution.py
@@ -13,6 +13,11 @@
 PAD = 256
 NQ = 4
 DEEP = 2
+PLANE = sorted(
+    [(dx, dy) for dx in range(NX) for dy in range(NY) if (dx, dy) != (0, 0)],
+    key=lambda o: -min(o[0], NX - o[0]) - min(o[1], NY - o[1]),
+)
+ALONG_Z = (4, 3, 5, 2, 6, 1, 7)
 F32, BF16 = jnp.float32, jnp.bfloat16
 HIGH = lax.Precision.HIGHEST
 MESH = pl.DeviceIdType.MESH
@@ -209,7 +214,7 @@
     def send_z(h):
         if h:
             left(zbuf.at[pl.ds(0, 7)], z_send.at[h - 1])
-        for d in range(1, NZ):
+        for d in ALONG_Z:
             there = (z + d) % NZ // 4
             send(
                 pack.at[there * NQ + h], zbuf.at[h * NZ + z], z_send.at[h], z_sem.at[h],
@@ -232,6 +237,7 @@
         hid_t[:, i * 256:(i + 1) * 256] = dot(hidden, pick).astype(BF16)
     send_z(1)
     pacc[...] = jnp.zeros_like(pacc)
+    pt_mine[...] = jnp.zeros_like(pt_mine)
     res_copy.wait()
     q_copy.wait()
 
@@ -321,7 +327,6 @@
         pltpu.make_async_copy(mer, mer_out, out_sem.at[0]).wait()
 
     add_left(blocks_out[-1])
-    pt_mine[...] = jnp.zeros_like(pt_mine)
     pt_mine[:, 0:ROWS] = pacc[...]
     send(pt_mine, pt_other, sends.at[0], b_sem.at[0], device(dz=4))
     later(pt_mine, 0)
@@ -337,9 +342,6 @@
     gram_c[0] = packed
     send(gram_c.at[0], gram_c.at[1], sends.at[1], gc_sem.at[0], sibling)
     later(gram_c.at[0], 1)
-    for d in range(1, 4):
-        send(pg.at[slot], pg.at[slot], sends.at[3], px_sem.at[0], device(dx=d))
-    later(pg.at[pl.ds(0, 3)], 3)
 
     hi = pt.astype(BF16)
     rest = pt - hi.astype(F32)
@@ -357,7 +359,7 @@
             wb[nb + 1] = total[:, 128:256]
             return carry
 
-        lax.fori_loop(0, 8, tile, 0, unroll=4)
+        lax.fori_loop(0, 8, tile, 0, unroll=True)
 
     for h in range(2):
         w_tiles(other * 32 + h * 16)
@@ -367,16 +369,17 @@
         )
         if h:
             continue
+        for d in range(1, 4):
+            send(pg.at[slot], pg.at[slot], sends.at[3], px_sem.at[0], device(dx=d))
+        later(pg.at[pl.ds(0, 3)], 3)
         arrived(gram_c.at[0], gc_sem.at[0])
         spot = x * 4 + y
         gram_p[spot] = gram_c[0] + gram_c[1]
-        for dx in range(NX):
-            for dy in range(NY):
-                if (dx, dy) != (0, 0):
-                    send(
-                        gram_p.at[spot], gram_p.at[spot], sends.at[4], gp_sem.at[0],
-                        device(dx=dx, dy=dy),
-                    )
+        for dx, dy in PLANE:
+            send(
+                gram_p.at[spot], gram_p.at[spot], sends.at[4], gp_sem.at[0],
+                device(dx=dx, dy=dy),
+            )
         later(gram_p.at[pl.ds(0, 15)], 4)
     later(wr, 2)
     places = (x, y)
@@ -386,7 +389,7 @@
         arrived(wr.at[pl.ds(h * 16, 16)], c1_sem.at[h])
         at = pl.ds(c * 32 + h * 16, 16)
         wb[at] = wb[at] + wr[pl.ds(h * 16, 16)]
-        for d in range(1, 4):
+        for d in (2, 1, 3):
             there = (places[h] + d) % 4
             send(
                 wb.at[pl.ds(c * 32 + h * 16 + there * 4, 4)], c2r.at[h * 4 + places[h]],
@@ -399,7 +402,7 @@
     for i in range(1, 16):
         total += gram_p[i]
     gram_z[z] = total
-    for d in range(1, NZ):
+    for d in ALONG_Z:
         send(gram_z.at[z], gram_z.at[z], sends.at[9], gz_sem.at[0], device(dz=d))
     later(gram_z.at[pl.ds(0, 7)], 9)
 
@@ -415,7 +418,7 @@
         for d in range(1, 4):
             total += c2r[h * 4 + (places[h] + d) % 4]
         w2[h] = total
-        for d in range(1, 4):
+        for d in (2, 1, 3):
             there = (places[1 - h] + d) % 4
             send(
                 w2.at[h, there], c3r.at[h * 4 + places[1 - h]],
@@ -440,7 +443,7 @@
         for d in range(1, 4):
             total += c3r[h * 4 + (places[1 - h] + d) % 4]
         zw[h * NZ + z] = (dot(inverse, total, precision=HIGH) * 0.5).astype(BF16)
-        for d in range(1, NZ):
+        for d in ALONG_Z:
             send(zw.at[h * NZ + z], zw.at[h * NZ + z], sends.at[10], zw_sem.at[h], device(dz=d))
     later(zw.at[pl.ds(0, 14)], 10)
 
@@ -451,13 +454,11 @@
         for i in range(1, NZ):
             total += zw[h * NZ + i].astype(F32)
         qt[h, mine] = total.astype(BF16)
-        for dx in range(NX):
-            for dy in range(NY):
-                if (dx, dy) != (0, 0):
-                    send(
-                        qt.at[h, mine], qt.at[h, mine], sends.at[11 + h],
-                        ag_sem.at[h * dx + h], device(dx=dx, dy=dy),
-                    )
+        for dx, dy in PLANE:
+            send(
+                qt.at[h, mine], qt.at[h, mine], sends.at[11 + h],
+                ag_sem.at[h * dx + h], device(dx=dx, dy=dy),
+            )
         later(qt.at[h, pl.ds(0, 15)], 11 + h)
 
     arrived(pg.at[pl.ds(0, 12)], pz_sem.at[0])

time: 95.9 us -> 93.2 us (0.972)
  Pallas kernels: 95.2 us -> 92.5 us
    pallas_call x1, Pallas kernels: 90.6 us -> 87.9 us  [exchange(): pl.pallas_call(main_kernel, out_shape=(jax.ShapeDtypeStruct((ROWS, D), BF...]
where the time goes in v2:
time: 93.2 us; the launch traced here: 93.1 us
  Pallas kernels  92.5 us (99%)
    pallas_call x1, Pallas kernels, exchange(): pl.pallas_call(main_kernel, out_shape=(jax.ShapeDtypeStruct((ROWS, D), BF...  87.9 us
    pallas_call x1, Pallas kernels, finish(): pl.pallas_call(final_kernel, out_shape=(jax.ShapeDtypeStruct((ROWS, D), B...  4.59 us

profile of v2, /device:TPU:1, one launch (start us, length us, event | category | flops | bytes accessed | tf_op | source)
XLA Modules:
  0.0 93.1 jit_solution(13787741814070995993)
XLA Ops:
  0.6 87.9 %exchange.1 = (bf16[224,8192]{1,0:T(8,128)(2,1)}, f32[32,7168]{1,0:T(8,128)}, bf16[2,32,32,128]{3,2,1,0:T(8,128)(2,1)}, bf16[224,128]{1,0:T(8,128)(2,1)}) custom-call(bf16[224,768]{1,0:T(8,128)(2,1)} %bitcast.10, bf16[12,4096]{1,0:T(8,128)(2,1)} %og_hbm.1, bf16[32,8192]{1,0:T(8,128)(2,1)} %bitcast.9, bf16[224,8192]{1,0:T(8,128)(2,1)} %bitcast.8), custom_call_target="tpu_custom_call" | custom-call | tf_op jit(solution)/shard_map/exchange/pallas_call | solution.py:505
  88.5 4.6 %finish.1 = (bf16[224,8192]{1,0:T(8,128)(2,1)}, f32[32,7168]{1,0:T(8,128)}, f32[32,128]{1,0:T(8,128)}) custom-call(bf16[224,8192]{1,0:T(8,128)(2,1)} %get-tuple-element.10.mer_hbm, f32[32,7168]{1,0:T(8,128)} %get-tuple-element.11.pb_hbm, bf16[2,32,32,128]{3,2,1,0:T(8,128)(2,1)} %get-tuple-element.12.qt_hbm, bf16[224,128]{1,0:T(8,128)(2,1)} %get-tuple-element.13.low_hbm), custom_call_target="tpu_custom_call" | custom-call | tf_op jit(solution)/shard_map/finish/pallas_call | solution.py:620

commit v3 on v2

--- a/solution.py
+++ b/solution.py
@@ -447,6 +447,16 @@
             send(zw.at[h * NZ + z], zw.at[h * NZ + z], sends.at[10], zw_sem.at[h], device(dz=d))
     later(zw.at[pl.ds(0, 14)], 10)
 
+    arrived(pg.at[pl.ds(0, 12)], pz_sem.at[0])
+    half = pg.at[pl.ds(c * 16, 16)]
+    send(half, half, sends.at[14], pc_sem.at[0], sibling)
+    later(half, 14)
+    own = dot(inverse, pg[slot], precision=HIGH)
+    own = jnp.concatenate([own, jnp.zeros((96, PAD), F32)], axis=0).T
+    low[...] = own[0:ROWS].astype(BF16)
+    low_copy = pltpu.make_async_copy(low, low_out, local_sem.at[0])
+    low_copy.start()
+
     mine = c * 16 + x * 4 + y
     for h in range(2):
         arrived(zw.at[pl.ds(0, 7)], zw_sem.at[h])
@@ -461,15 +471,6 @@
             )
         later(qt.at[h, pl.ds(0, 15)], 11 + h)
 
-    arrived(pg.at[pl.ds(0, 12)], pz_sem.at[0])
-    half = pg.at[pl.ds(c * 16, 16)]
-    send(half, half, sends.at[14], pc_sem.at[0], sibling)
-    later(half, 14)
-    own = dot(inverse, pg[slot], precision=HIGH)
-    own = jnp.concatenate([own, jnp.zeros((96, PAD), F32)], axis=0).T
-    low[...] = own[0:ROWS].astype(BF16)
-    low_copy = pltpu.make_async_copy(low, low_out, local_sem.at[0])
-    low_copy.start()
     arrived(half, pc_sem.at[0])
     for i in range(8):
         blocks = []

time: 93.2 us -> 93.2 us (level)
  no operation moved by 1% of the time
where the time goes in v3:
time: 93.2 us; the launch traced here: 93.1 us
  Pallas kernels  92.5 us (99%)
    pallas_call x1, Pallas kernels, exchange(): pl.pallas_call(main_kernel, out_shape=(jax.ShapeDtypeStruct((ROWS, D), BF...  87.9 us
    pallas_call x1, Pallas kernels, finish(): pl.pallas_call(final_kernel, out_shape=(jax.ShapeDtypeStruct((ROWS, D), B...  4.59 us

profile of v3, /device:TPU:1, one launch (start us, length us, event | category | flops | bytes accessed | tf_op | source)
XLA Modules:
  0.0 93.1 jit_solution(8450667964506972528)
XLA Ops:
  0.6 87.9 %exchange.1 = (bf16[224,8192]{1,0:T(8,128)(2,1)}, f32[32,7168]{1,0:T(8,128)}, bf16[2,32,32,128]{3,2,1,0:T(8,128)(2,1)}, bf16[224,128]{1,0:T(8,128)(2,1)}) custom-call(bf16[224,768]{1,0:T(8,128)(2,1)} %bitcast.10, bf16[12,4096]{1,0:T(8,128)(2,1)} %og_hbm.1, bf16[32,8192]{1,0:T(8,128)(2,1)} %bitcast.9, bf16[224,8192]{1,0:T(8,128)(2,1)} %bitcast.8), custom_call_target="tpu_custom_call" | custom-call | tf_op jit(solution)/shard_map/exchange/pallas_call | solution.py:506
  88.5 4.6 %finish.1 = (bf16[224,8192]{1,0:T(8,128)(2,1)}, f32[32,7168]{1,0:T(8,128)}, f32[32,128]{1,0:T(8,128)}) custom-call(bf16[224,8192]{1,0:T(8,128)(2,1)} %get-tuple-element.10.mer_hbm, f32[32,7168]{1,0:T(8,128)} %get-tuple-element.11.pb_hbm, bf16[2,32,32,128]{3,2,1,0:T(8,128)(2,1)} %get-tuple-element.12.qt_hbm, bf16[224,128]{1,0:T(8,128)(2,1)} %get-tuple-element.13.low_hbm), custom_call_target="tpu_custom_call" | custom-call | tf_op jit(solution)/shard_map/finish/pallas_call | solution.py:621

commit v4 on v3

--- a/solution.py
+++ b/solution.py
@@ -145,7 +145,7 @@
 def main_kernel(
     hid_hbm, og_hbm, q_hbm, res_hbm,
     mer_out, pb_out, qt_out, low_out,
-    hid, og, pack, zbuf, grads, hid_t, res, mer, qv, pacc, pt_mine, pt_other, pg, pb, low,
+    hid, og, pack, picks, zbuf, grads, hid_t, res, mer, qv, pacc, pt_mine, pt_other, pg, pb, low,
     wb, wr, c2r, w2, c3r, gram_c, gram_p, gram_z, zw, qt,
     z_send, z_sem, link_send, xy_sem, core_send, core_sem, sends, b_sem, gc_sem, c1_sem,
     gp_sem, c2_sem, c3_sem, gz_sem, zw_sem, pz_sem, px_sem, pc_sem, ag_sem, agc_sem,
@@ -236,6 +236,10 @@
         pick = one_hot(iota((TOK, 256), 0) == token)
         hid_t[:, i * 256:(i + 1) * 256] = dot(hidden, pick).astype(BF16)
     send_z(1)
+    r = iota((384, 1), 0)
+    g = jnp.where(r >= 96, 1, 0) + jnp.where(r >= 192, 1, 0) + jnp.where(r >= 288, 1, 0)
+    r = r - g * 96
+    picks[...] = one_hot(iota((384, 384), 1) == r + div12(r) * 36 + g * TOK_DEV)
     pacc[...] = jnp.zeros_like(pacc)
     pt_mine[...] = jnp.zeros_like(pt_mine)
     res_copy.wait()
@@ -276,12 +280,10 @@
         if h + 2 < NQ:
             send_z(h + 2)
         arrived(zbuf.at[pl.ds(0, 7)], z_sem.at[h])
-        packed = zbuf[h * NZ:(h + 1) * NZ].reshape(384, 128)
+        tokens = dot(picks[...], zbuf[h * NZ:(h + 1) * NZ].reshape(384, 128)).astype(BF16)
         row = pl.multiple_of(x * 192 + c * 96, 16)
         for g in range(4):
-            r, s = iota((96, 384), 0), iota((96, 384), 1)
-            pick = one_hot(s == r + div12(r) * 36 + g * TOK_DEV)
-            grads[y * NQ + h, pl.ds(row, 96), g * 128:(g + 1) * 128] = dot(pick, packed).astype(BF16)
+            grads[y * NQ + h, pl.ds(row, 96), g * 128:(g + 1) * 128] = tokens[g * 96:(g + 1) * 96]
         share(h, 0, 0)
 
     def forward(h, f, s):
@@ -487,15 +489,18 @@
     for dx in (0, 1, 3, 2):
         rows = qt.at[1, pl.ds(c * 16 + (x + 4 - dx) % 4 * 4, 4)]
         arrived(qt.at[1, pl.ds(0, 4 if dx else 3)], ag_sem.at[1 + dx])
-        send(rows, rows, sends.at[13], agc_sem.at[0], sibling)
+        send(rows, rows, sends.at[13], agc_sem.at[1], sibling)
     later(qt.at[0], 13)
-    arrived(qt.at[0], agc_sem.at[0])
-    qt_copy = pltpu.make_async_copy(qt, qt_out, local_sem.at[2])
-    qt_copy.start()
+    qt_copies = []
+    for h in range(2):
+        arrived(qt.at[0, pl.ds(0, 16)], agc_sem.at[h])
+        qt_copies.append(pltpu.make_async_copy(qt.at[h], qt_out.at[h], local_sem.at[2 + h]))
+        qt_copies[h].start()
     end()
     low_copy.wait()
     pb_copy.wait()
-    qt_copy.wait()
+    for copy in qt_copies:
+        copy.wait()
 
 
 def exchange(
@@ -517,6 +522,7 @@
             pltpu.VMEM((ROWS, TOK), BF16),
             pltpu.VMEM((TOK_DEV, 4096), BF16),
             pltpu.VMEM((8, 48, 128), BF16),
+            pltpu.VMEM((384, 384), BF16),
             pltpu.VMEM((NQ * NZ, 48, 128), BF16),
             pltpu.VMEM((4 * NQ, TOK, 512), BF16),
             pltpu.VMEM((ROWS, TOK), BF16),
@@ -558,7 +564,7 @@
             dma((1,)),
             dma((1,)),
             dma((5,)),
-            dma((1,)),
+            dma((2,)),
             dma((4,)),
             dma((1,)),
         ],

time: 93.2 us -> 93 us (level)
  no operation moved by 1% of the time
where the time goes in v4:
time: 93 us; the launch traced here: 92.9 us
  Pallas kernels  92.2 us (99%)
    pallas_call x1, Pallas kernels, exchange(): pl.pallas_call(main_kernel, out_shape=(jax.ShapeDtypeStruct((ROWS, D), BF...  87.7 us
    pallas_call x1, Pallas kernels, finish(): pl.pallas_call(final_kernel, out_shape=(jax.ShapeDtypeStruct((ROWS, D), B...  4.59 us

profile of v4, /device:TPU:1, one launch (start us, length us, event | category | flops | bytes accessed | tf_op | source)
XLA Modules:
  0.0 92.9 jit_solution(12791292519621501330)
XLA Ops:
  0.6 87.7 %exchange.1 = (bf16[224,8192]{1,0:T(8,128)(2,1)}, f32[32,7168]{1,0:T(8,128)}, bf16[2,32,32,128]{3,2,1,0:T(8,128)(2,1)}, bf16[224,128]{1,0:T(8,128)(2,1)}) custom-call(bf16[224,768]{1,0:T(8,128)(2,1)} %bitcast.10, bf16[12,4096]{1,0:T(8,128)(2,1)} %og_hbm.1, bf16[32,8192]{1,0:T(8,128)(2,1)} %bitcast.9, bf16[224,8192]{1,0:T(8,128)(2,1)} %bitcast.8), custom_call_target="tpu_custom_call" | custom-call | tf_op jit(solution)/shard_map/exchange/pallas_call | solution.py:511
  88.3 4.6 %finish.1 = (bf16[224,8192]{1,0:T(8,128)(2,1)}, f32[32,7168]{1,0:T(8,128)}, f32[32,128]{1,0:T(8,128)}) custom-call(bf16[224,8192]{1,0:T(8,128)(2,1)} %get-tuple-element.10.mer_hbm, f32[32,7168]{1,0:T(8,128)} %get-tuple-element.11.pb_hbm, bf16[2,32,32,128]{3,2,1,0:T(8,128)(2,1)} %get-tuple-element.12.qt_hbm, bf16[224,128]{1,0:T(8,128)(2,1)} %get-tuple-element.13.low_hbm), custom_call_target="tpu_custom_call" | custom-call | tf_op jit(solution)/shard_map/finish/pallas_call | solution.py:627
